TPU v7x, 32 devices: a whole 2x2x4 slice. The times are simulated.
32 devices in a mesh: rep: 2 (over x), region: 2 (over core), dev: 8 (over z, y).
Axes of the slice: x: 2, y: 2, z: 4, core: 2. Of those that a mesh axis runs over, the one named last changes fastest.
Arguments:
- queries: bfloat16 [32768, 512], P(('rep', 'region', 'dev')), parts along dimension 0, may hold values from -6 to 6
- tiles: bfloat16 [64, 1024, 1024], P(('rep', 'region', 'dev')), parts along dimension 0, may hold values from -0.09375 to 0.09375
- tile_cols: int32 [32, 2], P(('rep', 'region', 'dev')), parts along dimension 0, may hold values from 0 to 15, as said below
- tile_count: int32 [32], P(('rep', 'region', 'dev')), parts along dimension 0, may hold values from 1 to 2, as said below
Outputs:
- ranking: float32 [32768, 512], P(('rep', 'region', 'dev')), parts along dimension 0
There are 2 independent parts, one for each index of `rep`. A program takes and returns all parts, laid end to end along the dimension named above; each array names one. Nothing has to cross between parts.
Inputs may be any that keep to these rules, and one draw needn't show every extreme that they name: For row block r, tile_cols[r, s] is r, or r + k with 1 <= k <= 2 inside the same group of 8 blocks, or r + 8 when r < 8. `tile_count`: some row block has all 2 slots live in every draw.
All inputs are finite; a program needn't handle non-finite values.
Results may differ from a plain program's by a relative error of at most 0.002.
Values may be sent and summed in bfloat16 or wider, within the bound.
A program may use at most 128 MiB of HBM per device.

v0:
```python
import jax
import jax.numpy as jnp
from jax import lax
from jax.sharding import PartitionSpec as P

ITERS = 3
REACH = 2


damping = 0.8


def from_behind(block, axis, distance):
    devices = range(lax.axis_size(axis))
    route = [(i - distance, i) for i in devices if i - distance in devices]
    return lax.ppermute(block, axis, route)


def fetch_blocks(field):
    sources = [field]
    for distance in range(1, REACH + 1):
        sources.append(from_behind(field, "dev", -distance))
    sources.append(from_behind(field, "region", -1))
    return jnp.stack(sources)


def move_tiles(tiles, slot_bins, alive):
    held_tiles = []
    held_flags = []
    for distance in range(1, REACH + 2):
        keep = alive & (slot_bins == distance)
        masked = jnp.where(keep[:, None, None], tiles, jnp.zeros_like(tiles))
        flags = keep.astype(jnp.int32)
        if distance <= REACH:
            got_tiles, got_flags = from_behind((masked, flags), "dev", distance)
        else:
            got_tiles, got_flags = from_behind((masked, flags), "region", 1)
        held_tiles.append(got_tiles)
        held_flags.append(got_flags)
    return (jnp.concatenate(held_tiles, 0), jnp.concatenate(held_flags, 0))


def fields_behind(field):
    sources = []
    for distance in range(1, REACH + 1):
        sources.append(from_behind(field, "dev", distance))
    sources.append(from_behind(field, "region", 1))
    return jnp.stack(sources)


def on_device(queries, tiles, tile_cols, tile_count):
    dev_count = lax.axis_size("dev")
    slot_total = tiles.shape[0]
    own_block = lax.axis_index("region") * dev_count + lax.axis_index("dev")
    columns = tile_cols[0]
    live_count = tile_count[0]
    distance_all = columns - own_block
    slot_bins = jnp.where(distance_all > REACH, REACH + 1, distance_all)
    alive = jnp.arange(slot_total, dtype=jnp.int32) < live_count
    anchor = queries.astype(jnp.float32)
    field = queries
    update = anchor
    held_tiles, held_flags = move_tiles(tiles, slot_bins, alive)
    for iteration in range(ITERS):
        stacked = fetch_blocks(field)
        start_total = jnp.zeros(anchor.shape, jnp.float32)
        behind = fields_behind(field)

        def forward_only(slot_index, total):
            tile_now = lax.dynamic_index_in_dim(tiles, slot_index, 0, keepdims=False)
            slot_bin = lax.dynamic_index_in_dim(slot_bins, slot_index, 0, keepdims=False)
            source = lax.dynamic_index_in_dim(stacked, slot_bin, 0, keepdims=False)
            return total + jnp.dot(tile_now, source, preferred_element_type=jnp.float32)

        total = lax.fori_loop(0, live_count, forward_only, start_total)

        def transpose_side(item_index, total):
            flag = lax.dynamic_index_in_dim(held_flags, item_index, 0, keepdims=False)
            tile_now = lax.dynamic_index_in_dim(held_tiles, item_index, 0, keepdims=False)
            root = lax.dynamic_index_in_dim(behind, item_index // slot_total, 0, keepdims=False)

            def product(running):
                return running + lax.dot_general(
                    tile_now, root, (((0,), (0,)), ((), ())), preferred_element_type=jnp.float32
                )

            return lax.cond(flag > 0, product, lambda running: running, total)

        total = lax.fori_loop(0, held_flags.shape[0], transpose_side, total)
        update = damping * total + anchor
        field = update.astype(jnp.bfloat16)
    return update


def solution(mesh):
    return jax.shard_map(
        on_device,
        mesh=mesh,
        in_specs=(
            P(("rep", "region", "dev"), None),
            P(("rep", "region", "dev"), None, None),
            P(("rep", "region", "dev"), None),
            P(("rep", "region", "dev")),
        ),
        out_specs=P(("rep", "region", "dev"), None),
        check_vma=False,
    )
```

profile of v0, /device:TPU:15, one launch (start us, length us, event | category | flops | bytes accessed | tf_op | source)
XLA Modules:
  0.0 477.9 jit_solution(18421571366523776925)
XLA Ops:
  2.1 4.0 collective-permute-start.9
  7.5 6.4 %broadcast_select_fusion = (bf16[2,1024,1024]{2,1,0:T(8,128)(2,1)}, bf16[2,1024,1024]{2,1,0:T(8,128)(2,1)}, bf16[2,1024,1024]{2,1,0:T(8,128)(2,1)}) fusion(bf16[2,1024,1024]{2,1,0:T(8,128)(2,1)} %param.23, pred[2]{0:T(512)(128)(4,1)S(1)} %get-tuple-element.964, pred[2]{0:T(512)(128)(4,1)S(1)} %get-tuple-element.957, pred[2]{0:T(512)(128)(4,1)S(1)} %get-tuple-element.954), kind=kLoop, calls=%fused_computation.45 | loop fusion | flops 6291456 | bytes 16777222 | tf_op jit(solution)/shard_map/jit(_where)/select_n | solution.py:32
  16.2 4.2 collective-permute-start.7
  22.3 186.4 %collective-permute-done.4 = s32[2]{0:T(128)S(1)} collective-permute-done((s32[2]{0:T(128)S(1)}, s32[2]{0:T(128)S(1)}, u32[]{:S(2)}, u32[]{:S(2)}) %collective-permute-start.4) | collective-permute-done | bytes 40 | tf_op jit(solution)/shard_map/ppermute | solution.py:16
  222.6 19.4 %collective-permute-done.10 = bf16[1024,512]{1,0:T(8,128)(2,1)S(1)} collective-permute-done((bf16[1024,512]{1,0:T(8,128)(2,1)S(1)}, bf16[1024,512]{1,0:T(8,128)(2,1)S(1)}, u32[]{:S(2)}, u32[]{:S(2)}) %collective-permute-start.10) | collective-permute-done | bytes 1048608 | tf_op jit(solution)/shard_map/ppermute | solution.py:16
  244.8 5.2 %collective-permute-start.2 = (bf16[1024,512]{1,0:T(8,128)(2,1)S(1)}, bf16[1024,512]{1,0:T(8,128)(2,1)}, u32[]{:S(2)}, u32[]{:S(2)}) collective-permute-start(bf16[1024,512]{1,0:T(8,128)(2,1)S(1)} %copy-done), channel_id=1, source_target_pairs={{8,0},{9,1},{10,2},{11,3},{12,4},{13,5},{14,6},{15,7},{24,16},{25,... | collective-permute-start | bytes 3145736 | tf_op jit(solution)/shard_map/ppermute | solution.py:16
  250.1 3.2 pad_maximum_fusion.3
  253.3 13.0 %collective-permute-done.1 = bf16[1024,512]{1,0:T(8,128)(2,1)} collective-permute-done((bf16[1024,512]{1,0:T(8,128)(2,1)S(1)}, bf16[1024,512]{1,0:T(8,128)(2,1)}, u32[]{:S(2)}, u32[]{:S(2)}) %collective-permute-start.1) | collective-permute-done | bytes 1048608 | tf_op jit(solution)/shard_map/ppermute | solution.py:16
  266.3 3.6 pad_maximum_fusion
  270.1 13.5 %while.84 = (s32[]{:T(128)}, f32[1024,512]{1,0:T(8,128)S(1)}, s32[]{:T(128)}, bf16[2,1024,1024]{2,1,0:T(8,128)(2,1)}, s32[2]{0:T(128)S(1)}, /*index=5*/bf16[4,10...) while((s32[]{:T(128)}, f32[1024,512]{1,0:T(8,128)S(1)}, s32[]{:T(128)}, ...), condition=%wide.region_1.2_spmd, body=%wide.region_0.1_spmd.sunk | while | flops 1074266112 | bytes 7340221 | solution.py:75
  273.3 3.2 fusion.70
  279.8 3.2 fusion.70
  291.6 4.5 copy-done.1
  296.1 17.1 %while.85 = (s32[]{:T(128)}, f32[1024,512]{1,0:T(8,128)S(1)}, s32[6]{0:T(128)S(1)}, bf16[6,1024,1024]{2,1,0:T(8,128)(2,1)}, bf16[3,1024,512]{2,1,0:T(8,128)(2,1)}, /*index=5*/s32[]{:T(128)}, s32[1]{0:T(128)}) while((s32[]{:T(128)}, f32[1024,512]{1,0:T(8,128)S(1)}, s32[6]{0:T(128)S(1)}, bf16[6,1024,1024]{2,1,0:T(8,128)(2,1)}, ...), condition=%wide.region_5.6_spmd, body=%wide.region_2.5_spmd.sunk | while | flops 1074266112 | bytes 7340803 | solution.py:89
  320.7 4.3 collective-permute-start.15
  325.0 3.4 collective-permute-start.16
  328.4 27.7 %collective-permute-done.12 = bf16[1024,512]{1,0:T(8,128)(2,1)S(1)} collective-permute-done((bf16[1024,512]{1,0:T(8,128)(2,1)}, bf16[1024,512]{1,0:T(8,128)(2,1)S(1)}, u32[]{:S(2)}, u32[]{:S(2)}) %collective-permute-start.12) | collective-permute-done | bytes 1048608 | tf_op jit(solution)/shard_map/ppermute | solution.py:16
  357.4 3.4 pad_maximum_fusion.1
  361.1 13.1 %while.86 = (s32[]{:T(128)}, f32[1024,512]{1,0:T(8,128)S(1)}, s32[]{:T(128)}, bf16[2,1024,1024]{2,1,0:T(8,128)(2,1)}, s32[2]{0:T(128)S(1)}, /*index=5*/bf16[4,10...) while((s32[]{:T(128)}, f32[1024,512]{1,0:T(8,128)S(1)}, s32[]{:T(128)}, ...), condition=%wide.region_7.8_spmd, body=%wide.region_6.7_spmd.sunk | while | flops 1074266112 | bytes 7340221 | solution.py:75
  364.1 3.2 fusion.73
  370.3 3.2 fusion.73
  374.2 3.8 pad_maximum_fusion.4
  378.0 17.1 %while.87 = (s32[]{:T(128)}, f32[1024,512]{1,0:T(8,128)S(1)}, s32[6]{0:T(128)S(1)}, bf16[6,1024,1024]{2,1,0:T(8,128)(2,1)}, bf16[3,1024,512]{2,1,0:T(8,128)(2,1)}, /*index=5*/s32[]{:T(128)}, s32[1]{0:T(128)}) while((s32[]{:T(128)}, f32[1024,512]{1,0:T(8,128)S(1)}, s32[6]{0:T(128)S(1)}, bf16[6,1024,1024]{2,1,0:T(8,128)(2,1)}, ...), condition=%wide.region_11.12_spmd, body=%wide.region_8.11_spmd.sunk | while | flops 1074266112 | bytes 7340803 | solution.py:89
  402.6 4.3 collective-permute-start.21
  406.9 5.8 %collective-permute-start.22 = (bf16[1024,512]{1,0:T(8,128)(2,1)}, bf16[1024,512]{1,0:T(8,128)(2,1)}, u32[]{:S(2)}, u32[]{:S(2)}) collective-permute-start(bf16[1024,512]{1,0:T(8,128)(2,1)} %fusion.55), channel_id=1, source_target_pairs={{0,2},{1,3},{2,4},{3,5},{4,6},{5,7},{8,10},{9,11},{10,12},{11,13},... | collective-permute-start | bytes 3145736 | tf_op jit(solution)/shard_map/ppermute | solution.py:16
  412.8 24.2 %collective-permute-done.18 = bf16[1024,512]{1,0:T(8,128)(2,1)S(1)} collective-permute-done((bf16[1024,512]{1,0:T(8,128)(2,1)}, bf16[1024,512]{1,0:T(8,128)(2,1)S(1)}, u32[]{:S(2)}, u32[]{:S(2)}) %collective-permute-start.18) | collective-permute-done | bytes 1048608 | tf_op jit(solution)/shard_map/ppermute | solution.py:16
  438.2 3.4 pad_maximum_fusion.2
  441.9 13.3 %while.88 = (s32[]{:T(128)}, f32[1024,512]{1,0:T(8,128)S(1)}, s32[]{:T(128)}, bf16[2,1024,1024]{2,1,0:T(8,128)(2,1)}, s32[2]{0:T(128)S(1)}, /*index=5*/bf16[4,10...) while((s32[]{:T(128)}, f32[1024,512]{1,0:T(8,128)S(1)}, s32[]{:T(128)}, ...), condition=%wide.region_13.14_spmd, body=%wide.region_12.13_spmd.sunk | while | flops 1074266112 | bytes 7340221 | solution.py:75
  445.1 3.2 fusion.76
  451.3 3.2 fusion.76
  455.2 3.8 pad_maximum_fusion.5
  459.1 17.1 %while.89 = (s32[]{:T(128)}, f32[1024,512]{1,0:T(8,128)S(1)}, s32[6]{0:T(128)S(1)}, bf16[6,1024,1024]{2,1,0:T(8,128)(2,1)}, bf16[3,1024,512]{2,1,0:T(8,128)(2,1)}, /*index=5*/s32[]{:T(128)}, s32[1]{0:T(128)}) while((s32[]{:T(128)}, f32[1024,512]{1,0:T(8,128)S(1)}, s32[6]{0:T(128)S(1)}, bf16[6,1024,1024]{2,1,0:T(8,128)(2,1)}, ...), condition=%wide.region_17.18_spmd, body=%wide.region_14.17_spmd.sunk | while | flops 1074266112 | bytes 7340803 | solution.py:89
  (104 shorter events, 122.6 us)
Async XLA Ops:
  0.0 219.9 %collective-permute-start = (bf16[1024,512]{1,0:T(8,128)(2,1)}, bf16[1024,512]{1,0:T(8,128)(2,1)}, u32[]{:S(2)}, u32[]{:S(2)}) collective-permute-start(bf16[1024,512]{1,0:T(8,128)(2,1)} %param.22), channel_id=1, source_target_pairs={{1,0},{2,1},{3,2},{4,3},{5,4},{6,5},{7,6},{9,8},{10,9},{11,10},{12... | collective-permute-start | bytes 3145736 | tf_op jit(solution)/shard_map/ppermute | solution.py:16
  2.1 219.1 %collective-permute-start.9 = (bf16[1024,512]{1,0:T(8,128)(2,1)}, bf16[1024,512]{1,0:T(8,128)(2,1)S(1)}, u32[]{:S(2)}, u32[]{:S(2)}) collective-permute-start(bf16[1024,512]{1,0:T(8,128)(2,1)} %param.22), channel_id=1, source_target_pairs={{0,1},{1,2},{2,3},{3,4},{4,5},{5,6},{6,7},{8,9},{9,10},{10,11},{11... | collective-permute-start | bytes 3145736 | tf_op jit(solution)/shard_map/ppermute | solution.py:16
  7.5 209.2 %copy-start = (bf16[1024,512]{1,0:T(8,128)(2,1)S(1)}, bf16[1024,512]{1,0:T(8,128)(2,1)}, u32[]{:S(2)}) copy-start(bf16[1024,512]{1,0:T(8,128)(2,1)} %param.22) | copy-start | bytes 3145732
  13.9 269.7 %collective-permute-start.6 = (bf16[2,1024,1024]{2,1,0:T(8,128)(2,1)}, bf16[2,1024,1024]{2,1,0:T(8,128)(2,1)}, u32[]{:S(2)}, u32[]{:S(2)}) collective-permute-start(bf16[2,1024,1024]{2,1,0:T(8,128)(2,1)} %get-tuple-element.962), channel_id=1, source_target_pairs={{0,1},{1,2},{2,3},{3,4},{4,5},{5,6},{6,7},{8,9},{9,10},{10,11},{11... | collective-permute-start | bytes 12582920 | tf_op jit(solution)/shard_map/ppermute | solution.py:16
  16.2 270.1 %collective-permute-start.7 = (bf16[2,1024,1024]{2,1,0:T(8,128)(2,1)}, bf16[2,1024,1024]{2,1,0:T(8,128)(2,1)}, u32[]{:S(2)}, u32[]{:S(2)}) collective-permute-start(bf16[2,1024,1024]{2,1,0:T(8,128)(2,1)} %get-tuple-element.961), channel_id=1, source_target_pairs={{0,2},{1,3},{2,4},{3,5},{4,6},{5,7},{8,10},{9,11},{10,12},{11,13},... | collective-permute-start | bytes 12582920 | tf_op jit(solution)/shard_map/ppermute | solution.py:16
  20.4 188.4 %collective-permute-start.4 = (s32[2]{0:T(128)S(1)}, s32[2]{0:T(128)S(1)}, u32[]{:S(2)}, u32[]{:S(2)}) collective-permute-start(s32[2]{0:T(128)S(1)} %get-tuple-element.956), channel_id=1, source_target_pairs={{0,2},{1,3},{2,4},{3,5},{4,6},{5,7},{8,10},{9,11},{10,12},{11,13},... | collective-permute-start | bytes 32 | tf_op jit(solution)/shard_map/ppermute | solution.py:16
  208.8 3.7 collective-permute-start.5
  212.5 4.3 collective-permute-start.3
  216.7 25.2 %collective-permute-start.10 = (bf16[1024,512]{1,0:T(8,128)(2,1)S(1)}, bf16[1024,512]{1,0:T(8,128)(2,1)S(1)}, u32[]{:S(2)}, u32[]{:S(2)}) collective-permute-start(bf16[1024,512]{1,0:T(8,128)(2,1)S(1)} %copy-done), channel_id=1, source_target_pairs={{0,2},{1,3},{2,4},{3,5},{4,6},{5,7},{8,10},{9,11},{10,12},{11,13},... | collective-permute-start | bytes 3145736 | tf_op jit(solution)/shard_map/ppermute | solution.py:16
  219.9 23.9 %collective-permute-start.11 = (bf16[1024,512]{1,0:T(8,128)(2,1)S(1)}, bf16[1024,512]{1,0:T(8,128)(2,1)S(1)}, u32[]{:S(2)}, u32[]{:S(2)}) collective-permute-start(bf16[1024,512]{1,0:T(8,128)(2,1)S(1)} %copy-done), channel_id=1, source_target_pairs={{0,8},{1,9},{2,10},{3,11},{4,12},{5,13},{6,14},{7,15},{16,24},{17,... | collective-permute-start | bytes 3145736 | tf_op jit(solution)/shard_map/ppermute | solution.py:16
  221.3 67.7 %collective-permute-start.8 = (bf16[2,1024,1024]{2,1,0:T(8,128)(2,1)}, bf16[2,1024,1024]{2,1,0:T(8,128)(2,1)}, u32[]{:S(2)}, u32[]{:S(2)}) collective-permute-start(bf16[2,1024,1024]{2,1,0:T(8,128)(2,1)} %get-tuple-element.960), channel_id=1, source_target_pairs={{0,8},{1,9},{2,10},{3,11},{4,12},{5,13},{6,14},{7,15},{16,24},{17,... | collective-permute-start | bytes 12582920 | tf_op jit(solution)/shard_map/ppermute | solution.py:16
  241.9 24.4 %collective-permute-start.1 = (bf16[1024,512]{1,0:T(8,128)(2,1)S(1)}, bf16[1024,512]{1,0:T(8,128)(2,1)}, u32[]{:S(2)}, u32[]{:S(2)}) collective-permute-start(bf16[1024,512]{1,0:T(8,128)(2,1)S(1)} %copy-done), channel_id=1, source_target_pairs={{2,0},{3,1},{4,2},{5,3},{6,4},{7,5},{10,8},{11,9},{12,10},{13,11},... | collective-permute-start | bytes 3145736 | tf_op jit(solution)/shard_map/ppermute | solution.py:16
  243.8 1.0 copy-start.2
  244.8 21.5 %collective-permute-start.2 = (bf16[1024,512]{1,0:T(8,128)(2,1)S(1)}, bf16[1024,512]{1,0:T(8,128)(2,1)}, u32[]{:S(2)}, u32[]{:S(2)}) collective-permute-start(bf16[1024,512]{1,0:T(8,128)(2,1)S(1)} %copy-done), channel_id=1, source_target_pairs={{8,0},{9,1},{10,2},{11,3},{12,4},{13,5},{14,6},{15,7},{24,16},{25,... | collective-permute-start | bytes 3145736 | tf_op jit(solution)/shard_map/ppermute | solution.py:16
  291.6 4.5 copy-start.1
  314.6 41.5 %collective-permute-start.12 = (bf16[1024,512]{1,0:T(8,128)(2,1)}, bf16[1024,512]{1,0:T(8,128)(2,1)S(1)}, u32[]{:S(2)}, u32[]{:S(2)}) collective-permute-start(bf16[1024,512]{1,0:T(8,128)(2,1)} %fusion.54), channel_id=1, source_target_pairs={{1,0},{2,1},{3,2},{4,3},{5,4},{6,5},{7,6},{9,8},{10,9},{11,10},{12... | collective-permute-start | bytes 3145736 | tf_op jit(solution)/shard_map/ppermute | solution.py:16
  316.5 40.9 %collective-permute-start.13 = (bf16[1024,512]{1,0:T(8,128)(2,1)}, bf16[1024,512]{1,0:T(8,128)(2,1)S(1)}, u32[]{:S(2)}, u32[]{:S(2)}) collective-permute-start(bf16[1024,512]{1,0:T(8,128)(2,1)} %fusion.54), channel_id=1, source_target_pairs={{2,0},{3,1},{4,2},{5,3},{6,4},{7,5},{10,8},{11,9},{12,10},{13,11},... | collective-permute-start | bytes 3145736 | tf_op jit(solution)/shard_map/ppermute | solution.py:16
  318.4 39.0 %collective-permute-start.14 = (bf16[1024,512]{1,0:T(8,128)(2,1)}, bf16[1024,512]{1,0:T(8,128)(2,1)}, u32[]{:S(2)}, u32[]{:S(2)}) collective-permute-start(bf16[1024,512]{1,0:T(8,128)(2,1)} %fusion.54), channel_id=1, source_target_pairs={{8,0},{9,1},{10,2},{11,3},{12,4},{13,5},{14,6},{15,7},{24,16},{25,... | collective-permute-start | bytes 3145736 | tf_op jit(solution)/shard_map/ppermute | solution.py:16
  320.7 53.5 %collective-permute-start.15 = (bf16[1024,512]{1,0:T(8,128)(2,1)}, bf16[1024,512]{1,0:T(8,128)(2,1)}, u32[]{:S(2)}, u32[]{:S(2)}) collective-permute-start(bf16[1024,512]{1,0:T(8,128)(2,1)} %fusion.54), channel_id=1, source_target_pairs={{0,1},{1,2},{2,3},{3,4},{4,5},{5,6},{6,7},{8,9},{9,10},{10,11},{11... | collective-permute-start | bytes 3145736 | tf_op jit(solution)/shard_map/ppermute | solution.py:16
  325.0 49.2 %collective-permute-start.16 = (bf16[1024,512]{1,0:T(8,128)(2,1)}, bf16[1024,512]{1,0:T(8,128)(2,1)}, u32[]{:S(2)}, u32[]{:S(2)}) collective-permute-start(bf16[1024,512]{1,0:T(8,128)(2,1)} %fusion.54), channel_id=1, source_target_pairs={{0,2},{1,3},{2,4},{3,5},{4,6},{5,7},{8,10},{9,11},{10,12},{11,13},... | collective-permute-start | bytes 3145736 | tf_op jit(solution)/shard_map/ppermute | solution.py:16
  356.1 18.1 %collective-permute-start.17 = (bf16[1024,512]{1,0:T(8,128)(2,1)}, bf16[1024,512]{1,0:T(8,128)(2,1)}, u32[]{:S(2)}, u32[]{:S(2)}) collective-permute-start(bf16[1024,512]{1,0:T(8,128)(2,1)} %fusion.54), channel_id=1, source_target_pairs={{0,8},{1,9},{2,10},{3,11},{4,12},{5,13},{6,14},{7,15},{16,24},{17,... | collective-permute-start | bytes 3145736 | tf_op jit(solution)/shard_map/ppermute | solution.py:16
  396.5 40.4 %collective-permute-start.18 = (bf16[1024,512]{1,0:T(8,128)(2,1)}, bf16[1024,512]{1,0:T(8,128)(2,1)S(1)}, u32[]{:S(2)}, u32[]{:S(2)}) collective-permute-start(bf16[1024,512]{1,0:T(8,128)(2,1)} %fusion.55), channel_id=1, source_target_pairs={{1,0},{2,1},{3,2},{4,3},{5,4},{6,5},{7,6},{9,8},{10,9},{11,10},{12... | collective-permute-start | bytes 3145736 | tf_op jit(solution)/shard_map/ppermute | solution.py:16
  398.4 39.8 %collective-permute-start.19 = (bf16[1024,512]{1,0:T(8,128)(2,1)}, bf16[1024,512]{1,0:T(8,128)(2,1)S(1)}, u32[]{:S(2)}, u32[]{:S(2)}) collective-permute-start(bf16[1024,512]{1,0:T(8,128)(2,1)} %fusion.55), channel_id=1, source_target_pairs={{2,0},{3,1},{4,2},{5,3},{6,4},{7,5},{10,8},{11,9},{12,10},{13,11},... | collective-permute-start | bytes 3145736 | tf_op jit(solution)/shard_map/ppermute | solution.py:16
  400.3 37.9 %collective-permute-start.20 = (bf16[1024,512]{1,0:T(8,128)(2,1)}, bf16[1024,512]{1,0:T(8,128)(2,1)}, u32[]{:S(2)}, u32[]{:S(2)}) collective-permute-start(bf16[1024,512]{1,0:T(8,128)(2,1)} %fusion.55), channel_id=1, source_target_pairs={{8,0},{9,1},{10,2},{11,3},{12,4},{13,5},{14,6},{15,7},{24,16},{25,... | collective-permute-start | bytes 3145736 | tf_op jit(solution)/shard_map/ppermute | solution.py:16
  402.6 52.5 %collective-permute-start.21 = (bf16[1024,512]{1,0:T(8,128)(2,1)}, bf16[1024,512]{1,0:T(8,128)(2,1)}, u32[]{:S(2)}, u32[]{:S(2)}) collective-permute-start(bf16[1024,512]{1,0:T(8,128)(2,1)} %fusion.55), channel_id=1, source_target_pairs={{0,1},{1,2},{2,3},{3,4},{4,5},{5,6},{6,7},{8,9},{9,10},{10,11},{11... | collective-permute-start | bytes 3145736 | tf_op jit(solution)/shard_map/ppermute | solution.py:16
  406.9 48.3 %collective-permute-start.22 = (bf16[1024,512]{1,0:T(8,128)(2,1)}, bf16[1024,512]{1,0:T(8,128)(2,1)}, u32[]{:S(2)}, u32[]{:S(2)}) collective-permute-start(bf16[1024,512]{1,0:T(8,128)(2,1)} %fusion.55), channel_id=1, source_target_pairs={{0,2},{1,3},{2,4},{3,5},{4,6},{5,7},{8,10},{9,11},{10,12},{11,13},... | collective-permute-start | bytes 3145736 | tf_op jit(solution)/shard_map/ppermute | solution.py:16
  436.9 18.3 %collective-permute-start.23 = (bf16[1024,512]{1,0:T(8,128)(2,1)}, bf16[1024,512]{1,0:T(8,128)(2,1)}, u32[]{:S(2)}, u32[]{:S(2)}) collective-permute-start(bf16[1024,512]{1,0:T(8,128)(2,1)} %fusion.55), channel_id=1, source_target_pairs={{0,8},{1,9},{2,10},{3,11},{4,12},{5,13},{6,14},{7,15},{16,24},{17,... | collective-permute-start | bytes 3145736 | tf_op jit(solution)/shard_map/ppermute | solution.py:16
where the time goes:
time: 487 us; the launch traced here: 478 us
  waiting for transfers between devices  275 us (56%)
  starting transfers between devices  63.2 us (13%)
  matrix products  47.7 us (10%)
  other arithmetic  32.8 us (7%)
  loops' own time  29.5 us (6%)
  local copies, waits for them, and re-layouts  28.2 us (6%)
    ppermute x24, waiting for transfers between devices, from_behind(): return lax.ppermute(block, axis, route)  275 us
    ppermute x24, starting transfers between devices, from_behind(): return lax.ppermute(block, axis, route)  63.2 us
    dot_general x9, matrix products, product(): lax.dot_general(tile_now, root, (((0,), (0,)), ((), ())), preferred_eleme...  28.4 us
    dot_general x6, matrix products, forward_only(): return total + jnp.dot(tile_now, source, preferred_element_type=jnp.float32)  19.3 us
    another operation x3, loops' own time, on_device(): total = lax.fori_loop(0, live_count, forward_only, start_total)  17 us
    another operation x3, loops' own time, on_device(): total = lax.fori_loop(0, held_flags.shape[0], transpose_side, total)  12.1 us
    another operation x3, other arithmetic, fields_behind(): return jnp.stack(sources)  10.9 us
    unnamed x8, local copies, waits for them, and re-layouts  10.7 us
  transfers between devices with their start and end apart: 24, of which 7 were waited for; matrix products, arithmetic and copies ran while one was open for 10% of the time, Pallas kernels for 0%

commit v1 on v0

v1 whole, which is shorter than its diff:
```python
import functools

import jax
import jax.numpy as jnp
from jax import lax
from jax.experimental import pallas as pl
from jax.experimental.pallas import tpu as pltpu
from jax.sharding import PartitionSpec as P

ITERS = 3
REACH = 2
CHUNKS = 2
ROWS = 256
KINDS = REACH + 1

damping = 0.8

MESH = pl.DeviceIdType.MESH


def kernel(n, bins_ref, gates_ref, tiles_ref, q_ref, out_ref, *scratch):
    slots, tile, _ = tiles_ref.shape
    width = q_ref.shape[1] // CHUNKS
    steps = ITERS * CHUNKS
    wt_ref = scratch[0]
    srcs = scratch[1 : 1 + steps]
    gots = scratch[1 + steps : 1 + 2 * steps]
    puts = scratch[1 + 2 * steps : 1 + 3 * steps]
    send_sem, recv_sem = scratch[1 + 3 * steps :]

    rep = lax.axis_index("rep")
    region = lax.axis_index("region")
    me = lax.axis_index("dev")

    has_lower = [me >= d for d in range(1, REACH + 1)] + [region == 1]
    has_upper = [me + d < n for d in range(1, REACH + 1)] + [region == 0]
    lower = [(rep, region, me - d) for d in range(1, REACH + 1)] + [(rep, 0, me)]
    upper = [(rep, region, me + d) for d in range(1, REACH + 1)] + [(rep, 1, me)]

    barrier = pltpu.get_barrier_semaphore()
    count = jnp.int32(0)
    for there, device in list(zip(has_lower, lower)) + list(zip(has_upper, upper)):
        count = count + there.astype(jnp.int32)

        @pl.when(there)
        def _(device=device):
            pl.semaphore_signal(barrier, inc=1, device_id=device, device_id_type=MESH)

    for ch in range(CHUNKS):
        srcs[ch][0] = q_ref[:, ch * width : (ch + 1) * width]
    pl.semaphore_wait(barrier, count)

    def field_copy(step, k, device):
        return pltpu.make_async_remote_copy(
            src_ref=srcs[step].at[0],
            dst_ref=srcs[step].at[k + 1],
            send_sem=send_sem.at[step, k],
            recv_sem=recv_sem.at[step, k],
            device_id=device,
            device_id_type=MESH,
        )

    def product_copy(step, k, device):
        return pltpu.make_async_remote_copy(
            src_ref=puts[step].at[k],
            dst_ref=gots[step].at[k],
            send_sem=send_sem.at[step, KINDS + k],
            recv_sem=recv_sem.at[step, KINDS + k],
            device_id=device,
            device_id_type=MESH,
        )

    def send_fields(step):
        for k in range(KINDS):

            @pl.when(has_lower[k])
            def _(k=k):
                field_copy(step, k, lower[k]).start()

    def send_products(step):
        source = srcs[step]

        @pl.loop(0, tile // ROWS)
        def _(i):
            rows = pl.ds(pl.multiple_of(i * ROWS, ROWS), ROWS)
            parts = [
                jnp.dot(wt_ref[s, rows, :], source[0], preferred_element_type=jnp.float32)
                for s in range(slots)
            ]
            for k in range(KINDS):
                total = gates_ref[0, k + 1] * parts[0]
                for s in range(1, slots):
                    total = total + gates_ref[s, k + 1] * parts[s]
                puts[step][k, rows, :] = total.astype(jnp.bfloat16)

        for k in range(KINDS):

            @pl.when(has_upper[k])
            def _(k=k):
                product_copy(step, k, upper[k]).start()

    def finish(step):
        for k in range(KINDS):

            @pl.when(has_upper[k])
            def _(k=k):
                field_copy(step, k, upper[k]).wait_recv()

            @pl.when(has_lower[k])
            def _(k=k):
                product_copy(step, k, lower[k]).wait_recv()

        it, ch = divmod(step, CHUNKS)
        columns = pl.ds(ch * width, width)
        source = srcs[step]

        @pl.loop(0, tile // ROWS)
        def _(i):
            rows = pl.ds(pl.multiple_of(i * ROWS, ROWS), ROWS)
            total = jnp.zeros((ROWS, width), jnp.float32)
            for s in range(slots):
                live = gates_ref[s, KINDS + 1]
                total = total + live * jnp.dot(
                    tiles_ref[s, rows, :], source[bins_ref[s]], preferred_element_type=jnp.float32
                )
            for k in range(KINDS):
                landed = gots[step][k, rows, :].astype(jnp.float32)
                total = total + jnp.where(has_lower[k], landed, jnp.zeros_like(landed))
            update = damping * total + q_ref[rows, columns].astype(jnp.float32)
            if it == ITERS - 1:
                out_ref[rows, columns] = update
            else:
                srcs[step + CHUNKS][0, rows, :] = update.astype(jnp.bfloat16)

    for ch in range(CHUNKS):
        send_fields(ch)

    for s in range(slots):

        @pl.loop(0, tile // ROWS)
        def _(i, s=s):
            rows = pl.ds(pl.multiple_of(i * ROWS, ROWS), ROWS)
            wt_ref[s, rows, :] = tiles_ref[s, :, rows].T

    for ch in range(CHUNKS):
        send_products(ch)

    for step in range(steps):
        finish(step)
        if step + CHUNKS < steps:
            send_fields(step + CHUNKS)
            send_products(step + CHUNKS)

    for step in range(steps):
        for k in range(KINDS):

            @pl.when(has_lower[k])
            def _(step=step, k=k):
                field_copy(step, k, lower[k]).wait_send()

            @pl.when(has_upper[k])
            def _(step=step, k=k):
                product_copy(step, k, upper[k]).wait_send()


def on_device(queries, tiles, tile_cols, tile_count):
    n = lax.axis_size("dev")
    slots, tile, _ = tiles.shape
    cols = queries.shape[1]
    width = cols // CHUNKS
    steps = ITERS * CHUNKS
    own = lax.axis_index("region") * n + lax.axis_index("dev")
    distance = tile_cols[0] - own
    alive = jnp.arange(slots, dtype=jnp.int32) < tile_count[0]
    bins = jnp.where(distance > REACH, REACH + 1, distance)
    bins = jnp.where(alive, bins, 0).astype(jnp.int32)
    which = (bins[:, None] == jnp.arange(REACH + 2, dtype=jnp.int32)[None]) & alive[:, None]
    gates = jnp.concatenate([which, alive[:, None]], 1).astype(jnp.float32)

    vmem = pl.BlockSpec(memory_space=pltpu.VMEM)
    smem = pl.BlockSpec(memory_space=pltpu.SMEM)
    products = 2 * slots * ITERS
    return pl.pallas_call(
        functools.partial(kernel, n),
        out_shape=jax.ShapeDtypeStruct((tile, cols), jnp.float32),
        in_specs=[smem, smem, vmem, vmem],
        out_specs=vmem,
        scratch_shapes=[pltpu.VMEM((slots, tile, tile), jnp.bfloat16)]
        + [pltpu.VMEM((KINDS + 1, tile, width), jnp.bfloat16)] * steps
        + [pltpu.VMEM((KINDS, tile, width), jnp.bfloat16)] * (2 * steps)
        + [pltpu.SemaphoreType.DMA((steps, 2 * KINDS))] * 2,
        compiler_params=pltpu.CompilerParams(
            collective_id=0, has_side_effects=True, vmem_limit_bytes=58 * 2**20
        ),
        cost_estimate=pl.CostEstimate(
            flops=2 * products * tile * tile * cols,
            bytes_accessed=2 * tiles.size + 6 * tile * cols,
            transcendentals=0,
        ),
        name="diffuse",
    )(bins, gates, tiles, queries)


def solution(mesh):
    return jax.shard_map(
        on_device,
        mesh=mesh,
        in_specs=(
            P(("rep", "region", "dev"), None),
            P(("rep", "region", "dev"), None, None),
            P(("rep", "region", "dev"), None),
            P(("rep", "region", "dev")),
        ),
        out_specs=P(("rep", "region", "dev"), None),
        check_vma=False,
    )
```

time: 487 us -> 153 us (0.31); the launches traced: 478 us -> 152 us
  waiting for transfers between devices: 275 us -> 0 us
  Pallas kernels: 0 us -> 147 us
  starting transfers between devices: 63.2 us -> 0 us
  matrix products: 47.7 us -> 0 us
  other arithmetic: 32.8 us -> 1.39 us
  loops' own time: 29.5 us -> 0 us
  local copies, waits for them, and re-layouts: 28.2 us -> 3.08 us
    ppermute x24 -> x0, waiting for transfers between devices: 275 us -> none  [from_behind(): return lax.ppermute(block, axis, route)]
    pallas_call x0 -> x1, Pallas kernels: none -> 147 us  [on_device(): pl.pallas_call(functools.partial(kernel, n), out_shape=jax.ShapeDtypeStru...]
    ppermute x24 -> x0, starting transfers between devices: 63.2 us -> none  [from_behind(): return lax.ppermute(block, axis, route)]
    dot_general x15 -> x0, matrix products: 47.7 us -> none  [the longest x9 28.4 us: product(): lax.dot_general(tile_now, root, (((0,), (0,)), ((), ())), preferred_eleme...]
    another operation x24 -> x0, loops' own time: 29.5 us -> none  [the longest x3 17 us: on_device(): total = lax.fori_loop(0, live_count, forward_only, start_total)]
    another operation x6 -> x0, other arithmetic: 21.4 us -> none  [the longest x3 10.9 us: fields_behind(): return jnp.stack(sources)]
    dynamic_slice x24 -> x0, local copies, waits for them, and re-layouts: 14.1 us -> none  [the longest x18 10.5 us: transpose_side(): flag = lax.dynamic_index_in_dim(held_flags, item_index, 0, keepdims=False)]
    unnamed x8 -> x3, local copies, waits for them, and re-layouts: 10.7 us -> 3.08 us
  transfers between devices with their start and end apart: 24 -> 0, of which waited for: 7 -> 0; matrix products, arithmetic and copies ran while one was open for 10% -> 0% of each run, Pallas kernels for 0% -> 0%
where the time goes in v1:
time: 153 us; the launch traced here: 152 us
  Pallas kernels  147 us (96%)
  local copies, waits for them, and re-layouts  3.08 us (2%)
    pallas_call x1, Pallas kernels, on_device(): pl.pallas_call(functools.partial(kernel, n), out_shape=jax.ShapeDtypeStru...  147 us
    unnamed x3, local copies, waits for them, and re-layouts  3.08 us

profile of v1, /device:TPU:15, one launch (start us, length us, event | category | flops | bytes accessed | tf_op | source)
XLA Modules:
  0.0 151.8 jit_solution(14083828349915802443)
XLA Ops:
  0.7 0.7 fusion.bins_ref
  1.3 0.0 copy-start
  1.3 0.1 compare_and_fusion
  1.4 0.6 add_convert_fusion.gates_ref
  2.0 0.0 copy-done
  2.0 146.7 %diffuse.1 = f32[1024,512]{1,0:T(8,128)} custom-call(s32[2]{0:T(128)} %copy-done, f32[2,5]{1,0:T(2,128)} %add_convert_fusion.gates_ref, bf16[2,1024,1024]{2,1,0:T(8,128)(2,1)} %tiles_ref.1, bf16[1024,512]{1,0:T(8,128)(2,1)} %q_ref.1), custom_call_target="tpu_custom_call" | custom-call | flops 12884901888 | bytes 7340032 | tf_op jit(solution)/shard_map/diffuse/pallas_call | solution.py:183
  148.7 3.1 %copy.7 = f32[1024,512]{1,0:T(8,128)} copy(f32[1024,512]{1,0:T(8,128)} %diffuse.1) | data formatting | bytes 4194304
  (2 shorter events, 0.0 us)
Async XLA Ops:
  1.3 0.7 copy-start

commit v2 on v1

--- a/solution.py
+++ b/solution.py
@@ -18,24 +18,40 @@
 MESH = pl.DeviceIdType.MESH
 
 
-def kernel(n, bins_ref, gates_ref, tiles_ref, q_ref, out_ref, *scratch):
-    slots, tile, _ = tiles_ref.shape
+def kernel(n, cols_ref, count_ref, tiles_hbm, q_ref, out_ref, *scratch):
+    slots, tile, _ = tiles_hbm.shape
     width = q_ref.shape[1] // CHUNKS
     steps = ITERS * CHUNKS
-    wt_ref = scratch[0]
-    srcs = scratch[1 : 1 + steps]
-    gots = scratch[1 + steps : 1 + 2 * steps]
-    puts = scratch[1 + 2 * steps : 1 + 3 * steps]
-    send_sem, recv_sem = scratch[1 + 3 * steps :]
+    tiles_ref, wt_ref = scratch[:2]
+    srcs = scratch[2 : 2 + steps]
+    gots = scratch[2 + steps : 2 + 2 * steps]
+    puts = scratch[2 + 2 * steps : 2 + 3 * steps]
+    send_sem, recv_sem, tile_sem = scratch[2 + 3 * steps :]
+    fetches = [
+        pltpu.make_async_copy(tiles_hbm.at[s], tiles_ref.at[s], tile_sem.at[s])
+        for s in range(slots)
+    ]
 
     rep = lax.axis_index("rep")
     region = lax.axis_index("region")
     me = lax.axis_index("dev")
+
+    bins, gates = [], []
+    for s in range(slots):
+        distance = cols_ref[0, s] - (region * n + me)
+        live = s < count_ref[0]
+        place = jnp.where(distance > REACH, REACH + 1, distance)
+        bins.append(jnp.where(live, place, 0))
+        alive = jnp.where(live, 1.0, 0.0).astype(jnp.float32)
+        gates.append([jnp.where(place == k, alive, 0.0) for k in range(KINDS + 1)] + [alive])
 
     has_lower = [me >= d for d in range(1, REACH + 1)] + [region == 1]
     has_upper = [me + d < n for d in range(1, REACH + 1)] + [region == 0]
     lower = [(rep, region, me - d) for d in range(1, REACH + 1)] + [(rep, 0, me)]
     upper = [(rep, region, me + d) for d in range(1, REACH + 1)] + [(rep, 1, me)]
+
+    for fetch in fetches:
+        fetch.start()
 
     barrier = pltpu.get_barrier_semaphore()
     count = jnp.int32(0)
@@ -88,9 +104,9 @@
                 for s in range(slots)
             ]
             for k in range(KINDS):
-                total = gates_ref[0, k + 1] * parts[0]
+                total = gates[0][k + 1] * parts[0]
                 for s in range(1, slots):
-                    total = total + gates_ref[s, k + 1] * parts[s]
+                    total = total + gates[s][k + 1] * parts[s]
                 puts[step][k, rows, :] = total.astype(jnp.bfloat16)
 
         for k in range(KINDS):
@@ -119,9 +135,9 @@
             rows = pl.ds(pl.multiple_of(i * ROWS, ROWS), ROWS)
             total = jnp.zeros((ROWS, width), jnp.float32)
             for s in range(slots):
-                live = gates_ref[s, KINDS + 1]
+                live = gates[s][KINDS + 1]
                 total = total + live * jnp.dot(
-                    tiles_ref[s, rows, :], source[bins_ref[s]], preferred_element_type=jnp.float32
+                    tiles_ref[s, rows, :], source[bins[s]], preferred_element_type=jnp.float32
                 )
             for k in range(KINDS):
                 landed = gots[step][k, rows, :].astype(jnp.float32)
@@ -136,6 +152,7 @@
         send_fields(ch)
 
     for s in range(slots):
+        fetches[s].wait()
 
         @pl.loop(0, tile // ROWS)
         def _(i, s=s):
@@ -169,26 +186,19 @@
     cols = queries.shape[1]
     width = cols // CHUNKS
     steps = ITERS * CHUNKS
-    own = lax.axis_index("region") * n + lax.axis_index("dev")
-    distance = tile_cols[0] - own
-    alive = jnp.arange(slots, dtype=jnp.int32) < tile_count[0]
-    bins = jnp.where(distance > REACH, REACH + 1, distance)
-    bins = jnp.where(alive, bins, 0).astype(jnp.int32)
-    which = (bins[:, None] == jnp.arange(REACH + 2, dtype=jnp.int32)[None]) & alive[:, None]
-    gates = jnp.concatenate([which, alive[:, None]], 1).astype(jnp.float32)
-
     vmem = pl.BlockSpec(memory_space=pltpu.VMEM)
     smem = pl.BlockSpec(memory_space=pltpu.SMEM)
     products = 2 * slots * ITERS
     return pl.pallas_call(
         functools.partial(kernel, n),
         out_shape=jax.ShapeDtypeStruct((tile, cols), jnp.float32),
-        in_specs=[smem, smem, vmem, vmem],
+        in_specs=[smem, smem, pl.BlockSpec(memory_space=pl.ANY), vmem],
         out_specs=vmem,
-        scratch_shapes=[pltpu.VMEM((slots, tile, tile), jnp.bfloat16)]
+        scratch_shapes=[pltpu.VMEM((slots, tile, tile), jnp.bfloat16)] * 2
         + [pltpu.VMEM((KINDS + 1, tile, width), jnp.bfloat16)] * steps
         + [pltpu.VMEM((KINDS, tile, width), jnp.bfloat16)] * (2 * steps)
-        + [pltpu.SemaphoreType.DMA((steps, 2 * KINDS))] * 2,
+        + [pltpu.SemaphoreType.DMA((steps, 2 * KINDS))] * 2
+        + [pltpu.SemaphoreType.DMA((slots,))],
         compiler_params=pltpu.CompilerParams(
             collective_id=0, has_side_effects=True, vmem_limit_bytes=58 * 2**20
         ),
@@ -198,7 +208,7 @@
             transcendentals=0,
         ),
         name="diffuse",
-    )(bins, gates, tiles, queries)
+    )(tile_cols, tile_count, tiles, queries)
 
 
 def solution(mesh):

time: 153 us -> 150 us (0.980)
    unnamed x3 -> x1, local copies, waits for them, and re-layouts: 3.08 us -> 3.08 us
where the time goes in v2:
time: 150 us
  Pallas kernels  146 us (97%)
  local copies, waits for them, and re-layouts  3.08 us (2%)
    pallas_call x1, Pallas kernels, on_device(): pl.pallas_call(functools.partial(kernel, n), out_shape=jax.ShapeDtypeStru...  146 us
    unnamed x1, local copies, waits for them, and re-layouts  3.08 us

profile of v2, /device:TPU:15, one launch (start us, length us, event | category | flops | bytes accessed | tf_op | source)
XLA Modules:
  0.0 149.7 jit_solution(17060543808637742697)
XLA Ops:
  0.7 146.0 %diffuse.1 = f32[1024,512]{1,0:T(8,128)} custom-call(s32[1,2]{1,0:T(1,128)} %cols_ref.1, s32[1]{0:T(128)S(6)} %copy.6.count_ref, bf16[2,1024,1024]{2,1,0:T(8,128)(2,1)} %tiles_hbm.1, bf16[1024,512]{1,0:T(8,128)(2,1)} %q_ref.1), custom_call_target="tpu_custom_call" | custom-call | flops 12884901888 | bytes 7340032 | tf_op jit(solution)/shard_map/diffuse/pallas_call | solution.py:192
  146.6 3.1 %copy.7 = f32[1024,512]{1,0:T(8,128)} copy(f32[1024,512]{1,0:T(8,128)} %diffuse.1) | data formatting | bytes 4194304

commit v3 on v2

--- a/solution.py
+++ b/solution.py
@@ -18,7 +18,7 @@
 MESH = pl.DeviceIdType.MESH
 
 
-def kernel(n, cols_ref, count_ref, tiles_hbm, q_ref, out_ref, *scratch):
+def kernel(n, cols_ref, count_ref, tiles_hbm, q_ref, out_hbm, *scratch):
     slots, tile, _ = tiles_hbm.shape
     width = q_ref.shape[1] // CHUNKS
     steps = ITERS * CHUNKS
@@ -26,7 +26,8 @@
     srcs = scratch[2 : 2 + steps]
     gots = scratch[2 + steps : 2 + 2 * steps]
     puts = scratch[2 + 2 * steps : 2 + 3 * steps]
-    send_sem, recv_sem, tile_sem = scratch[2 + 3 * steps :]
+    sums = scratch[2 + 3 * steps : 2 + 3 * steps + CHUNKS]
+    send_sem, recv_sem, tile_sem, out_sem = scratch[2 + 3 * steps + CHUNKS :]
     fetches = [
         pltpu.make_async_copy(tiles_hbm.at[s], tiles_ref.at[s], tile_sem.at[s])
         for s in range(slots)
@@ -115,20 +116,21 @@
             def _(k=k):
                 product_copy(step, k, upper[k]).start()
 
+    def result_copy(ch):
+        return pltpu.make_async_copy(
+            sums[ch], out_hbm.at[:, pl.ds(ch * width, width)], out_sem.at[ch]
+        )
+
     def finish(step):
-        for k in range(KINDS):
-
-            @pl.when(has_upper[k])
-            def _(k=k):
-                field_copy(step, k, upper[k]).wait_recv()
-
-            @pl.when(has_lower[k])
-            def _(k=k):
-                product_copy(step, k, lower[k]).wait_recv()
-
         it, ch = divmod(step, CHUNKS)
         columns = pl.ds(ch * width, width)
         source = srcs[step]
+
+        for k in range(KINDS):
+
+            @pl.when(has_upper[k])
+            def _(k=k):
+                field_copy(step, k, upper[k]).wait_recv()
 
         @pl.loop(0, tile // ROWS)
         def _(i):
@@ -139,14 +141,29 @@
                 total = total + live * jnp.dot(
                     tiles_ref[s, rows, :], source[bins[s]], preferred_element_type=jnp.float32
                 )
+            sums[ch][rows, :] = total
+
+        for k in range(KINDS):
+
+            @pl.when(has_lower[k])
+            def _(k=k):
+                product_copy(step, k, lower[k]).wait_recv()
+
+        @pl.loop(0, tile // ROWS)
+        def _(i):
+            rows = pl.ds(pl.multiple_of(i * ROWS, ROWS), ROWS)
+            total = sums[ch][rows, :]
             for k in range(KINDS):
                 landed = gots[step][k, rows, :].astype(jnp.float32)
                 total = total + jnp.where(has_lower[k], landed, jnp.zeros_like(landed))
             update = damping * total + q_ref[rows, columns].astype(jnp.float32)
             if it == ITERS - 1:
-                out_ref[rows, columns] = update
+                sums[ch][rows, :] = update
             else:
                 srcs[step + CHUNKS][0, rows, :] = update.astype(jnp.bfloat16)
+
+        if it == ITERS - 1:
+            result_copy(ch).start()
 
     for ch in range(CHUNKS):
         send_fields(ch)
@@ -178,6 +195,9 @@
             @pl.when(has_upper[k])
             def _(step=step, k=k):
                 product_copy(step, k, upper[k]).wait_send()
+
+    for ch in range(CHUNKS):
+        result_copy(ch).wait()
 
 
 def on_device(queries, tiles, tile_cols, tile_count):
@@ -193,12 +213,13 @@
         functools.partial(kernel, n),
         out_shape=jax.ShapeDtypeStruct((tile, cols), jnp.float32),
         in_specs=[smem, smem, pl.BlockSpec(memory_space=pl.ANY), vmem],
-        out_specs=vmem,
+        out_specs=pl.BlockSpec(memory_space=pl.ANY),
         scratch_shapes=[pltpu.VMEM((slots, tile, tile), jnp.bfloat16)] * 2
         + [pltpu.VMEM((KINDS + 1, tile, width), jnp.bfloat16)] * steps
         + [pltpu.VMEM((KINDS, tile, width), jnp.bfloat16)] * (2 * steps)
+        + [pltpu.VMEM((tile, width), jnp.float32)] * CHUNKS
         + [pltpu.SemaphoreType.DMA((steps, 2 * KINDS))] * 2
-        + [pltpu.SemaphoreType.DMA((slots,))],
+        + [pltpu.SemaphoreType.DMA((slots,)), pltpu.SemaphoreType.DMA((CHUNKS,))],
         compiler_params=pltpu.CompilerParams(
             collective_id=0, has_side_effects=True, vmem_limit_bytes=58 * 2**20
         ),

time: 150 us -> 149 us (level)
  Pallas kernels: 146 us -> 144 us
    pallas_call x1, Pallas kernels: 146 us -> 144 us  [on_device(): pl.pallas_call(functools.partial(kernel, n), out_shape=jax.ShapeDtypeStru...]
where the time goes in v3:
time: 149 us; the launch traced here: 148 us
  Pallas kernels  144 us (97%)
  local copies, waits for them, and re-layouts  3.08 us (2%)
    pallas_call x1, Pallas kernels, on_device(): pl.pallas_call(functools.partial(kernel, n), out_shape=jax.ShapeDtypeStru...  144 us
    unnamed x1, local copies, waits for them, and re-layouts  3.08 us

profile of v3, /device:TPU:15, one launch (start us, length us, event | category | flops | bytes accessed | tf_op | source)
XLA Modules:
  0.0 147.9 jit_solution(14950827529942335706)
XLA Ops:
  0.7 144.2 %diffuse.1 = f32[1024,512]{1,0:T(8,128)} custom-call(s32[1,2]{1,0:T(1,128)} %cols_ref.1, s32[1]{0:T(128)S(6)} %copy.6.count_ref, bf16[2,1024,1024]{2,1,0:T(8,128)(2,1)} %tiles_hbm.1, bf16[1024,512]{1,0:T(8,128)(2,1)} %q_ref.1), custom_call_target="tpu_custom_call" | custom-call | flops 12884901888 | bytes 7340032 | tf_op jit(solution)/shard_map/diffuse/pallas_call | solution.py:212
  144.8 3.1 %copy.7 = f32[1024,512]{1,0:T(8,128)} copy(f32[1024,512]{1,0:T(8,128)} %diffuse.1) | data formatting | bytes 4194304

commit v4 on v3

--- a/solution.py
+++ b/solution.py
@@ -10,7 +10,7 @@
 ITERS = 3
 REACH = 2
 CHUNKS = 2
-ROWS = 256
+ROWS = 512
 KINDS = REACH + 1
 
 damping = 0.8

time: 149 us -> 149 us (level)
  no operation moved by 1% of the time
where the time goes in v4:
time: 149 us; the launch traced here: 147 us
  Pallas kernels  144 us (97%)
  local copies, waits for them, and re-layouts  3.08 us (2%)
    pallas_call x1, Pallas kernels, on_device(): pl.pallas_call(functools.partial(kernel, n), out_shape=jax.ShapeDtypeStru...  144 us
    unnamed x1, local copies, waits for them, and re-layouts  3.08 us

profile of v4, /device:TPU:15, one launch (start us, length us, event | category | flops | bytes accessed | tf_op | source)
XLA Modules:
  0.0 147.3 jit_solution(6174619869225730564)
XLA Ops:
  0.7 143.6 %diffuse.1 = f32[1024,512]{1,0:T(8,128)} custom-call(s32[1,2]{1,0:T(1,128)} %cols_ref.1, s32[1]{0:T(128)S(6)} %copy.6.count_ref, bf16[2,1024,1024]{2,1,0:T(8,128)(2,1)} %tiles_hbm.1, bf16[1024,512]{1,0:T(8,128)(2,1)} %q_ref.1), custom_call_target="tpu_custom_call" | custom-call | flops 12884901888 | bytes 7340032 | tf_op jit(solution)/shard_map/diffuse/pallas_call | solution.py:212
  144.3 3.1 %copy.7 = f32[1024,512]{1,0:T(8,128)} copy(f32[1024,512]{1,0:T(8,128)} %diffuse.1) | data formatting | bytes 4194304
